TPU v7x, 32 devices: a whole 2x2x4 slice. The times are simulated.
32 devices in a mesh: dp: 2 (over y), pipe: 4 (over x, core), tensor: 4 (over z).
Axes of the slice: x: 2, y: 2, z: 4, core: 2. Of those that a mesh axis runs over, the one named last changes fastest.
Arguments:
- tokens: bfloat16 [1024, 8192], P(('dp', 'tensor'), 'pipe'), parts along dimension 0, may hold values from -6 to 6
- gate_weight: bfloat16 [8192, 28672], P('pipe', 'tensor'), may hold values from -0.0625 to 0.0625
- up_weight: bfloat16 [8192, 28672], P('pipe', 'tensor'), may hold values from -0.0625 to 0.0625
- down_weight: bfloat16 [28672, 8192], P('tensor', 'pipe'), may hold values from -0.03125 to 0.03125
Outputs:
- mixed: bfloat16 [1024, 8192], P(('dp', 'tensor'), 'pipe'), parts along dimension 0
There are 2 independent parts, one for each index of `dp`. A program takes and returns all parts, laid end to end along the dimension named above; an argument that names none is the same for every part. Nothing has to cross between parts.
All inputs are finite; a program needn't handle non-finite values.
Results may differ from a plain program's by a relative error of at most 0.015.
Values may be sent and summed in bfloat16 or wider, within the bound.
No kernel may reach another device: no remote copies, remote signals or barrier semaphores. Data moves between devices by JAX's collectives and lax.ppermute only.
A program may use at most 256 MiB of HBM per device.

v0:
```python
import jax
import jax.numpy as jnp
from jax import lax
from jax.experimental import pallas as pl
from jax.experimental.pallas import tpu as pltpu
from jax.sharding import PartitionSpec as P

BF16, F32 = jnp.bfloat16, jnp.float32
MIB = 1 << 20
ANY = pl.BlockSpec(memory_space=pl.ANY)


def block_of(size, most):
    return max(b for b in range(128, most + 1, 128) if size % b == 0)


def params(mib):
    return pltpu.CompilerParams(vmem_limit_bytes=mib * MIB, dimension_semantics=("arbitrary",))


def cut_order(bits):
    order = [0]
    for bit in reversed(range(bits)):
        order = order + [j | 1 << bit for j in order]
    return order


def first_dots(shards, weights, bits, after):
    rows, depth = shards[0].shape
    width = weights[0].shape[1]
    n, g, k = 1 << bits, len(shards), len(weights)
    r, m = rows // n, len(shards) * rows
    step = block_of(width, 512)
    order = cut_order(bits)

    def kernel(*refs):
        x, w = refs[:g], refs[g : g + k]
        keep, send, held = refs[-3:]

        @pl.when(pl.program_id(0) == 0)
        def _():
            me = lax.axis_index("pipe")
            for at, j in enumerate(order):
                start = pl.multiple_of((me ^ j) * r, r)
                for i in range(g):
                    held[(at * g + i) * r : (at * g + i + 1) * r, :] = x[i][pl.ds(start, r), :]

        for i in range(k):
            part = jnp.dot(held[...], w[i][...], preferred_element_type=F32).astype(BF16)
            keep[i] = part[: m // 2]
            send[i] = part[m // 2 :]

    out = jax.ShapeDtypeStruct((k, m // 2, width), BF16)
    return pl.pallas_call(
        kernel,
        grid=(width // step,),
        in_specs=[pl.BlockSpec((rows, depth), lambda c: (0, 0))] * g
        + [pl.BlockSpec((depth, step), lambda c: (0, c))] * k
        + [ANY] * len(after),
        out_specs=[pl.BlockSpec((k, m // 2, step), lambda c: (0, 0, c))] * 2,
        out_shape=[out, out],
        scratch_shapes=[pltpu.VMEM((m, depth), BF16)],
        compiler_params=params(48),
        cost_estimate=pl.CostEstimate(
            flops=2 * k * m * depth * width, bytes_accessed=2 * k * depth * width, transcendentals=0
        ),
        name="first_dots",
    )(*shards, *weights, *after)


def fold(keep, got, after):
    k, m, width = keep.shape
    step = block_of(width, 2048)

    def kernel(*refs):
        a, b = refs[:2]
        stay, send = refs[-2:]
        for i in range(k):
            total = (a[i].astype(F32) + b[i].astype(F32)).astype(BF16)
            stay[i] = total[: m // 2]
            send[i] = total[m // 2 :]

    out = jax.ShapeDtypeStruct((k, m // 2, width), BF16)
    return pl.pallas_call(
        kernel,
        grid=(width // step,),
        in_specs=[pl.BlockSpec((k, m, step), lambda c: (0, 0, c))] * 2 + [ANY] * len(after),
        out_specs=[pl.BlockSpec((k, m // 2, step), lambda c: (0, 0, c))] * 2,
        out_shape=[out, out],
        compiler_params=params(32),
        cost_estimate=pl.CostEstimate(flops=k * m * width, bytes_accessed=6 * k * m * width, transcendentals=0),
        name="fold",
    )(keep, got, *after)


def activate(pairs, after):
    m, width = pairs[0][0].shape[1:]
    flat = [a for pair in pairs for a in pair]
    step = block_of(width, 2048)

    def kernel(*refs):
        out = refs[-1]
        sums = []
        for i in range(len(pairs)):
            a, b = refs[2 * i], refs[2 * i + 1]
            sums += [a[j].astype(F32) + b[j].astype(F32) for j in range(a.shape[0])]
        gate, up = sums
        out[...] = (gate / (1.0 + jnp.exp(-gate)) * up).astype(BF16)

    return pl.pallas_call(
        kernel,
        grid=(width // step,),
        in_specs=[pl.BlockSpec((a.shape[0], m, step), lambda c: (0, 0, c)) for a in flat] + [ANY] * len(after),
        out_specs=pl.BlockSpec((m, step), lambda c: (0, c)),
        out_shape=jax.ShapeDtypeStruct((m, width), BF16),
        compiler_params=params(32),
        cost_estimate=pl.CostEstimate(flops=8 * m * width, bytes_accessed=10 * m * width, transcendentals=m * width),
        name="activate",
    )(*flat, *after)


def last_dot(pieces, weight, g, after):
    n = len(pieces)
    m1, depth = pieces[0].shape
    width = weight.shape[1]
    r, m = m1 // g, m1 * n
    step = block_of(depth, 512)

    def kernel(*refs):
        h, w = refs[:n], refs[n]
        outs, total = refs[-1 - g : -1], refs[-1]
        c = pl.program_id(0)
        rows = jnp.concatenate([p[...] for p in h], axis=0)
        term = jnp.dot(rows, w[...], preferred_element_type=F32)

        @pl.when(c == 0)
        def _():
            total[...] = term

        @pl.when(c > 0)
        def _():
            total[...] += term

        @pl.when(c == pl.num_programs(0) - 1)
        def _():
            me = lax.axis_index("pipe")
            for j in range(n):
                start = pl.multiple_of((me ^ j) * r, r)
                for i in range(g):
                    at = (j * g + i) * r
                    outs[i][pl.ds(start, r), :] = total[at : at + r, :].astype(BF16)

    return pl.pallas_call(
        kernel,
        grid=(depth // step,),
        in_specs=[pl.BlockSpec((m1, step), lambda c: (0, c))] * n
        + [pl.BlockSpec((step, width), lambda c: (c, 0))]
        + [ANY] * len(after),
        out_specs=[pl.BlockSpec((r * n, width), lambda c: (0, 0))] * g,
        out_shape=[jax.ShapeDtypeStruct((r * n, width), BF16)] * g,
        scratch_shapes=[pltpu.VMEM((m, width), F32)],
        compiler_params=params(48),
        cost_estimate=pl.CostEstimate(flops=2 * m * depth * width, bytes_accessed=2 * depth * width, transcendentals=0),
        name="last_dot",
    )(*pieces, weight, *after)


def solution(mesh):
    n_pipe, n_tensor = mesh.shape["pipe"], mesh.shape["tensor"]
    bits = n_pipe.bit_length() - 1
    assert n_pipe == 1 << bits and bits >= 1
    ring = [(i, (i + 1) % n_tensor) for i in range(n_tensor)]

    def hop(value):
        return lax.ppermute(value, "tensor", ring)

    def swap(value, bit):
        return lax.ppermute(value, "pipe", [(i, i ^ (1 << bit)) for i in range(n_pipe)])

    def gather(own):
        pieces = {0: own}
        for bit in reversed(range(bits)):
            for j in list(pieces):
                pieces[j | 1 << bit] = swap(pieces[j], bit)
        return [pieces[j] for j in range(n_pipe)]

    def shards(tokens, gate_weight, up_weight, down_weight):
        held = [tokens]
        for _ in range(n_tensor - 1):
            held.append(hop(held[-1]))
        last = None

        def after():
            return [] if last is None else [last]

        def dots(chunk, weights):
            nonlocal last
            keep, send = first_dots([held[i] for i in chunk], weights, bits, after())
            last = send
            return keep, swap(send, 0)

        def folds(keep, got):
            nonlocal last
            for bit in range(1, bits):
                keep, send = fold(keep, got, after())
                last = send
                got = swap(send, bit)
            return keep, got

        def act(*pairs):
            nonlocal last
            last = activate(pairs, after())
            return gather(last)

        def down(pieces, chunk):
            nonlocal last
            out = last_dot(pieces, down_weight, len(chunk), after())
            last = out[0]
            return out

        first, end = [0], [n_tensor - 1]
        middle = [list(range(1, n_tensor - 1))[i : i + 2] for i in range(0, n_tensor - 2, 2)]
        terms = {}
        gate = dots(first, [gate_weight])
        up = dots(first, [up_weight])
        gate = folds(*gate)
        up = folds(*up)
        waiting = [(first, (gate, up))]
        for chunk in middle + [end]:
            both = dots(chunk, [gate_weight, up_weight])
            c, pairs = waiting.pop()
            hidden = act(*pairs)
            both = folds(*both)
            waiting.append((chunk, (both,)))
            for i, t in zip(c, down(hidden, c)):
                terms[i] = t
        c, pairs = waiting.pop()
        for i, t in zip(c, down(act(*pairs), c)):
            terms[i] = t
        total = terms[1].astype(F32)
        for i in list(range(2, n_tensor)) + [0]:
            total = hop(total.astype(BF16)).astype(F32) + terms[i].astype(F32)
        return (tokens.astype(F32) + total).astype(BF16)

    return jax.shard_map(
        shards,
        mesh=mesh,
        in_specs=(
            P(("dp", "tensor"), "pipe"),
            P("pipe", "tensor"),
            P("pipe", "tensor"),
            P("tensor", "pipe"),
        ),
        out_specs=P(("dp", "tensor"), "pipe"),
        check_vma=False,
    )
```

profile of v0, /device:TPU:0, one launch (start us, length us, event | category | flops | bytes accessed | tf_op | source)
XLA Modules:
  0.0 258.1 jit_solution(14704725103223897330)
XLA Ops:
  0.0 3.0 %collective-permute-start = (bf16[128,2048]{1,0:T(8,128)(2,1)}, bf16[128,2048]{1,0:T(8,128)(2,1)S(1)}, u32[]{:S(2)}, u32[]{:S(2)}) collective-permute-start(bf16[128,2048]{1,0:T(8,128)(2,1)} %refs_0_.3), channel_id=1, source_target_pairs={{0,1},{1,2},{2,3},{3,0},{4,5},{5,6},{6,7},{7,4},{8,9},{9,10},{10,1... | collective-permute-start | bytes 1572872 | tf_op jit(solution)/shard_map/ppermute | solution.py:175
  3.0 1.1 copy-done
  4.1 16.0 %first_dots.4 = (bf16[1,64,7168]{2,1,0:T(8,128)(2,1)S(1)}, bf16[1,64,7168]{2,1,0:T(8,128)(2,1)S(1)}) custom-call(bf16[128,2048]{1,0:T(8,128)(2,1)S(1)} %copy-done, bf16[2048,7168]{1,0:T(8,128)(2,1)} %refs_1_.5), custom_call_target="tpu_custom_call" | custom-call | flops 3758096384 | bytes 29360128 | tf_op jit(solution)/shard_map/first_dots/pallas_call | solution.py:54
  20.1 0.1 collective-permute-start.3
  20.2 16.0 %first_dots.5 = (bf16[1,64,7168]{2,1,0:T(8,128)(2,1)S(1)}, bf16[1,64,7168]{2,1,0:T(8,128)(2,1)S(1)}) custom-call(bf16[128,2048]{1,0:T(8,128)(2,1)S(1)} %copy-done, bf16[2048,7168]{1,0:T(8,128)(2,1)} %refs_2_.3, bf16[1,64,7168]{2,1,0:T(8,128)(2,1)S(1)} %get-tuple-element.23.refs_2_), custom_call_target="tpu_custom_call" | custom-call | flops 3758096384 | bytes 29360128 | tf_op jit(solution)/shard_map/first_dots/pallas_call | solution.py:54
  36.2 0.5 collective-permute-start.2
  36.8 0.0 collective-permute-done.refs_0_
  36.8 1.6 collective-permute-start.1
  38.3 0.0 collective-permute-done.3.refs_1_
  38.3 0.5 fold.4
  38.8 0.0 collective-permute-done.2.refs_1_
  38.9 0.5 fold.5
  39.4 13.1 %collective-permute-done.1.refs_1_ = bf16[128,2048]{1,0:T(8,128)(2,1)S(1)} collective-permute-done((bf16[128,2048]{1,0:T(8,128)(2,1)S(1)}, bf16[128,2048]{1,0:T(8,128)(2,1)S(1)}, u32[]{:S(2)}, u32[]{:S(2)}) %collective-permute-start.1) | collective-permute-done | bytes 524320 | tf_op jit(solution)/shard_map/ppermute | solution.py:175
  52.5 28.2 %first_dots.6 = (bf16[2,128,7168]{2,1,0:T(8,128)(2,1)S(1)}, bf16[2,128,7168]{2,1,0:T(8,128)(2,1)}) custom-call(bf16[128,2048]{1,0:T(8,128)(2,1)S(1)} %collective-permute-done.refs_0_, bf16[128,2048]{1,0:T(8,128)(2,1)S(1)} %collective-permute-done.1.refs_1_, bf16[2048,7168]{1,0:T(8,128)(2,1)} %refs_1_.5, bf16[2048,7168]{1,0:T(8,128)(2,1)} %refs_2_.3, ...), custom_call_target="tpu_custom_call" | custom-call | flops 15032385536 | bytes 58720256 | tf_op jit(solution)/shard_map/first_dots/pallas_call | solution.py:54
  80.7 0.0 collective-permute-start.4
  80.7 1.5 collective-permute-start.6
  82.1 0.5 collective-permute-start.5
  82.7 11.3 %collective-permute-done.6.refs_3_ = bf16[1,32,7168]{2,1,0:T(8,128)(2,1)S(1)} collective-permute-done((bf16[1,32,7168]{2,1,0:T(8,128)(2,1)S(1)}, bf16[1,32,7168]{2,1,0:T(8,128)(2,1)S(1)}, u32[]{:S(2)}, u32[]{:S(2)}) %collective-permute-start.6) | collective-permute-done | bytes 458784 | tf_op jit(solution)/shard_map/ppermute | solution.py:178
  94.0 9.4 %collective-permute-done.5.refs_1_ = bf16[1,32,7168]{2,1,0:T(8,128)(2,1)S(1)} collective-permute-done((bf16[1,32,7168]{2,1,0:T(8,128)(2,1)S(1)}, bf16[1,32,7168]{2,1,0:T(8,128)(2,1)S(1)}, u32[]{:S(2)}, u32[]{:S(2)}) %collective-permute-start.5) | collective-permute-done | bytes 458784 | tf_op jit(solution)/shard_map/ppermute | solution.py:178
  103.4 2.0 copy-done.2
  105.5 0.7 activate.3.refs_2_.refs_0_
  106.2 1.6 collective-permute-start.10
  107.7 0.0 collective-permute-done.4.refs_1_
  107.7 1.6 fold.6
  109.4 0.6 collective-permute-start.7
  110.0 0.0 collective-permute-start.9
  110.0 9.7 %collective-permute-done.10.refs_2_ = bf16[32,7168]{1,0:T(8,128)(2,1)S(1)} collective-permute-done((bf16[32,7168]{1,0:T(8,128)(2,1)S(1)}, bf16[32,7168]{1,0:T(8,128)(2,1)S(1)}, u32[]{:S(2)}, u32[]{:S(2)}) %collective-permute-start.10) | collective-permute-done | bytes 458784 | tf_op jit(solution)/shard_map/ppermute | solution.py:178
  119.7 0.0 collective-permute-start.11
  119.7 0.0 collective-permute-start.8
  119.7 0.0 collective-permute-done.9.refs_1_
  119.7 1.8 collective-permute-done.11.refs_3_
  121.5 16.8 %last_dot.3.refs_3_ = bf16[128,2048]{1,0:T(8,128)(2,1)S(1)} custom-call(bf16[32,7168]{1,0:T(8,128)(2,1)S(1)} %activate.3.refs_2_.refs_0_, bf16[32,7168]{1,0:T(8,128)(2,1)S(1)} %collective-permute-done.9.refs_1_, bf16[32,7168]{1,0:T(8,128)(2,1)S(1)} %collective-permute-done.10.refs_2_, bf16[32,7168]{1,0:T(8,128)(2,1)S(1)} %collective-permute-done.11.refs_3_, ...), custom_call_target="tpu_custom_call" | custom-call | flops 3758096384 | bytes 29360128 | tf_op jit(solution)/shard_map/last_dot/pallas_call | solution.py:153
  138.3 0.0 collective-permute-done.8.refs_0_
  138.3 23.4 %first_dots.7 = (bf16[2,64,7168]{2,1,0:T(8,128)(2,1)S(1)}, bf16[2,64,7168]{2,1,0:T(8,128)(2,1)S(1)}) custom-call(bf16[128,2048]{1,0:T(8,128)(2,1)S(1)} %collective-permute-done.8.refs_0_, bf16[2048,7168]{1,0:T(8,128)(2,1)} %refs_1_.5, bf16[2048,7168]{1,0:T(8,128)(2,1)} %refs_2_.3, bf16[128,2048]{1,0:T(8,128)(2,1)S(1)} %last_dot.3.refs_3_), custom_call_target="tpu_custom_call" | custom-call | flops 7516192768 | bytes 58720256 | tf_op jit(solution)/shard_map/first_dots/pallas_call | solution.py:54
  161.7 0.2 collective-permute-start.15
  161.9 0.0 collective-permute-done.7.refs_1_
  161.9 1.2 activate.4.refs_2_.refs_0_
  163.1 1.6 collective-permute-start.13
  164.7 0.1 collective-permute-start.12
  164.7 21.0 %collective-permute-done.13.refs_2_ = bf16[64,7168]{1,0:T(8,128)(2,1)S(1)} collective-permute-done((bf16[64,7168]{1,0:T(8,128)(2,1)S(1)}, bf16[64,7168]{1,0:T(8,128)(2,1)S(1)}, u32[]{:S(2)}, u32[]{:S(2)}) %collective-permute-start.13) | collective-permute-done | bytes 917536 | tf_op jit(solution)/shard_map/ppermute | solution.py:178
  185.8 0.0 collective-permute-start.14
  185.8 0.0 collective-permute-done.15.refs_1_
  185.8 0.9 fold.7
  186.7 1.6 collective-permute-start.18
  188.2 0.0 collective-permute-done.12.refs_1_
  188.2 0.0 collective-permute-done.14.refs_3_
  188.3 19.4 %last_dot.4 = (bf16[128,2048]{1,0:T(8,128)(2,1)S(1)}, bf16[128,2048]{1,0:T(8,128)(2,1)S(1)}) custom-call(bf16[64,7168]{1,0:T(8,128)(2,1)S(1)} %activate.4.refs_2_.refs_0_, bf16[64,7168]{1,0:T(8,128)(2,1)S(1)} %collective-permute-done.12.refs_1_, bf16[64,7168]{1,0:T(8,128)(2,1)S(1)} %collective-permute-done.13.refs_2_, ...), custom_call_target="tpu_custom_call" | custom-call | flops 7516192768 | bytes 29360128 | tf_op jit(solution)/shard_map/last_dot/pallas_call | solution.py:153
  207.7 0.1 collective-permute-start.16
  207.8 1.7 collective-permute-done.18.refs_1_
  209.5 0.7 activate.5.refs_0_.refs_5_
  210.2 1.6 collective-permute-start.20
  211.7 10.7 %collective-permute-done.20.refs_2_ = bf16[32,7168]{1,0:T(8,128)(2,1)S(1)} collective-permute-done((bf16[32,7168]{1,0:T(8,128)(2,1)S(1)}, bf16[32,7168]{1,0:T(8,128)(2,1)S(1)}, u32[]{:S(2)}, u32[]{:S(2)}) %collective-permute-start.20) | collective-permute-done | bytes 458784 | tf_op jit(solution)/shard_map/ppermute | solution.py:178
  222.4 0.0 collective-permute-start.21
  222.4 1.2 collective-permute-done.16
  223.6 0.1 add_convert_fusion.2
  223.7 0.0 copy-start.1
  223.7 0.1 collective-permute-start.17
  223.8 0.4 collective-permute-done.21.refs_3_
  224.2 16.8 %last_dot.5 = bf16[128,2048]{1,0:T(8,128)(2,1)S(1)} custom-call(bf16[32,7168]{1,0:T(8,128)(2,1)S(1)} %activate.5.refs_0_.refs_5_, bf16[32,7168]{1,0:T(8,128)(2,1)S(1)} %collective-permute-done.19.refs_1_, bf16[32,7168]{1,0:T(8,128)(2,1)S(1)} %collective-permute-done.20.refs_2_, bf16[32,7168]{1,0:T(8,128)(2,1)S(1)} %collective-permute-done.21.refs_3_, ...), custom_call_target="tpu_custom_call" | custom-call | flops 3758096384 | bytes 29360128 | tf_op jit(solution)/shard_map/last_dot/pallas_call | solution.py:153
  241.1 0.0 collective-permute-done.17
  241.1 0.1 add_convert_fusion.1
  241.2 0.1 collective-permute-start.22
  241.3 15.7 %collective-permute-done.22 = bf16[128,2048]{1,0:T(8,128)(2,1)S(1)} collective-permute-done((bf16[128,2048]{1,0:T(8,128)(2,1)S(1)}, bf16[128,2048]{1,0:T(8,128)(2,1)S(1)}, u32[]{:S(2)}, u32[]{:S(2)}) %collective-permute-start.22) | collective-permute-done | bytes 524320 | tf_op jit(solution)/shard_map/ppermute | solution.py:175
  257.0 1.0 add_convert_fusion
  (5 shorter events, 0.0 us)
Async XLA Ops:
  0.0 36.8 %collective-permute-start = (bf16[128,2048]{1,0:T(8,128)(2,1)}, bf16[128,2048]{1,0:T(8,128)(2,1)S(1)}, u32[]{:S(2)}, u32[]{:S(2)}) collective-permute-start(bf16[128,2048]{1,0:T(8,128)(2,1)} %refs_0_.3), channel_id=1, source_target_pairs={{0,1},{1,2},{2,3},{3,0},{4,5},{5,6},{6,7},{7,4},{8,9},{9,10},{10,1... | collective-permute-start | bytes 1572872 | tf_op jit(solution)/shard_map/ppermute | solution.py:175
  3.0 1.1 copy-start
  20.1 18.2 %collective-permute-start.3 = (bf16[1,64,7168]{2,1,0:T(8,128)(2,1)S(1)}, bf16[1,64,7168]{2,1,0:T(8,128)(2,1)S(1)}, u32[]{:S(2)}, u32[]{:S(2)}) collective-permute-start(bf16[1,64,7168]{2,1,0:T(8,128)(2,1)S(1)} %get-tuple-element.23.refs_2_), channel_id=1, source_target_pairs={{0,4},{4,0},{8,12},{12,8},{1,5},{5,1},{9,13},{13,9},{2,6},{6,2},{1... | collective-permute-start | bytes 2752520 | tf_op jit(solution)/shard_map/ppermute | solution.py:178
  36.2 2.6 %collective-permute-start.2 = (bf16[1,64,7168]{2,1,0:T(8,128)(2,1)S(1)}, bf16[1,64,7168]{2,1,0:T(8,128)(2,1)S(1)}, u32[]{:S(2)}, u32[]{:S(2)}) collective-permute-start(bf16[1,64,7168]{2,1,0:T(8,128)(2,1)S(1)} %get-tuple-element.25.refs_2_), channel_id=1, source_target_pairs={{0,4},{4,0},{8,12},{12,8},{1,5},{5,1},{9,13},{13,9},{2,6},{6,2},{1... | collective-permute-start | bytes 2752520 | tf_op jit(solution)/shard_map/ppermute | solution.py:178
  36.8 15.7 %collective-permute-start.1 = (bf16[128,2048]{1,0:T(8,128)(2,1)S(1)}, bf16[128,2048]{1,0:T(8,128)(2,1)S(1)}, u32[]{:S(2)}, u32[]{:S(2)}) collective-permute-start(bf16[128,2048]{1,0:T(8,128)(2,1)S(1)} %collective-permute-done.refs_0_), channel_id=1, source_target_pairs={{0,1},{1,2},{2,3},{3,0},{4,5},{5,6},{6,7},{7,4},{8,9},{9,10},{10,1... | collective-permute-start | bytes 1572872 | tf_op jit(solution)/shard_map/ppermute | solution.py:175
  80.7 27.1 %collective-permute-start.4 = (bf16[2,128,7168]{2,1,0:T(8,128)(2,1)}, bf16[2,128,7168]{2,1,0:T(8,128)(2,1)S(1)}, u32[]{:S(2)}, u32[]{:S(2)}) collective-permute-start(bf16[2,128,7168]{2,1,0:T(8,128)(2,1)} %get-tuple-element.30.refs_4_), channel_id=1, source_target_pairs={{0,4},{4,0},{8,12},{12,8},{1,5},{5,1},{9,13},{13,9},{2,6},{6,2},{1... | collective-permute-start | bytes 11010056 | tf_op jit(solution)/shard_map/ppermute | solution.py:178
  80.7 13.3 %collective-permute-start.6 = (bf16[1,32,7168]{2,1,0:T(8,128)(2,1)S(1)}, bf16[1,32,7168]{2,1,0:T(8,128)(2,1)S(1)}, u32[]{:S(2)}, u32[]{:S(2)}) collective-permute-start(bf16[1,32,7168]{2,1,0:T(8,128)(2,1)S(1)} %get-tuple-element.28.refs_4_), channel_id=1, source_target_pairs={{0,8},{4,12},{8,0},{12,4},{1,9},{5,13},{9,1},{13,5},{2,10},{6,14},... | collective-permute-start | bytes 1376264 | tf_op jit(solution)/shard_map/ppermute | solution.py:178
  82.1 21.3 %collective-permute-start.5 = (bf16[1,32,7168]{2,1,0:T(8,128)(2,1)S(1)}, bf16[1,32,7168]{2,1,0:T(8,128)(2,1)S(1)}, u32[]{:S(2)}, u32[]{:S(2)}) collective-permute-start(bf16[1,32,7168]{2,1,0:T(8,128)(2,1)S(1)} %get-tuple-element.27.refs_2_), channel_id=1, source_target_pairs={{0,8},{4,12},{8,0},{12,4},{1,9},{5,13},{9,1},{13,5},{2,10},{6,14},... | collective-permute-start | bytes 1376264 | tf_op jit(solution)/shard_map/ppermute | solution.py:178
  103.4 2.0 copy-start.2
  106.2 13.5 %collective-permute-start.10 = (bf16[32,7168]{1,0:T(8,128)(2,1)S(1)}, bf16[32,7168]{1,0:T(8,128)(2,1)S(1)}, u32[]{:S(2)}, u32[]{:S(2)}) collective-permute-start(bf16[32,7168]{1,0:T(8,128)(2,1)S(1)} %activate.3.refs_2_.refs_0_), channel_id=1, source_target_pairs={{0,8},{4,12},{8,0},{12,4},{1,9},{5,13},{9,1},{13,5},{2,10},{6,14},... | collective-permute-start | bytes 1376264 | tf_op jit(solution)/shard_map/ppermute | solution.py:178
  109.4 52.5 %collective-permute-start.7 = (bf16[2,64,7168]{2,1,0:T(8,128)(2,1)S(1)}, bf16[2,64,7168]{2,1,0:T(8,128)(2,1)S(1)}, u32[]{:S(2)}, u32[]{:S(2)}) collective-permute-start(bf16[2,64,7168]{2,1,0:T(8,128)(2,1)S(1)} %get-tuple-element.34.refs_5_), channel_id=1, source_target_pairs={{0,8},{4,12},{8,0},{12,4},{1,9},{5,13},{9,1},{13,5},{2,10},{6,14},... | collective-permute-start | bytes 5505032 | tf_op jit(solution)/shard_map/ppermute | solution.py:178
  110.0 9.7 %collective-permute-start.9 = (bf16[32,7168]{1,0:T(8,128)(2,1)S(1)}, bf16[32,7168]{1,0:T(8,128)(2,1)S(1)}, u32[]{:S(2)}, u32[]{:S(2)}) collective-permute-start(bf16[32,7168]{1,0:T(8,128)(2,1)S(1)} %activate.3.refs_2_.refs_0_), channel_id=1, source_target_pairs={{0,4},{4,0},{8,12},{12,8},{1,5},{5,1},{9,13},{13,9},{2,6},{6,2},{1... | collective-permute-start | bytes 1376264 | tf_op jit(solution)/shard_map/ppermute | solution.py:178
  119.7 1.8 collective-permute-start.11
  119.7 18.7 %collective-permute-start.8 = (bf16[128,2048]{1,0:T(8,128)(2,1)S(1)}, bf16[128,2048]{1,0:T(8,128)(2,1)S(1)}, u32[]{:S(2)}, u32[]{:S(2)}) collective-permute-start(bf16[128,2048]{1,0:T(8,128)(2,1)S(1)} %collective-permute-done.1.refs_1_), channel_id=1, source_target_pairs={{0,1},{1,2},{2,3},{3,0},{4,5},{5,6},{6,7},{7,4},{8,9},{9,10},{10,1... | collective-permute-start | bytes 1572872 | tf_op jit(solution)/shard_map/ppermute | solution.py:175
  161.7 24.1 %collective-permute-start.15 = (bf16[2,64,7168]{2,1,0:T(8,128)(2,1)S(1)}, bf16[2,64,7168]{2,1,0:T(8,128)(2,1)S(1)}, u32[]{:S(2)}, u32[]{:S(2)}) collective-permute-start(bf16[2,64,7168]{2,1,0:T(8,128)(2,1)S(1)} %get-tuple-element.35.refs_2_), channel_id=1, source_target_pairs={{0,4},{4,0},{8,12},{12,8},{1,5},{5,1},{9,13},{13,9},{2,6},{6,2},{1... | collective-permute-start | bytes 5505032 | tf_op jit(solution)/shard_map/ppermute | solution.py:178
  163.1 22.7 %collective-permute-start.13 = (bf16[64,7168]{1,0:T(8,128)(2,1)S(1)}, bf16[64,7168]{1,0:T(8,128)(2,1)S(1)}, u32[]{:S(2)}, u32[]{:S(2)}) collective-permute-start(bf16[64,7168]{1,0:T(8,128)(2,1)S(1)} %activate.4.refs_2_.refs_0_), channel_id=1, source_target_pairs={{0,8},{4,12},{8,0},{12,4},{1,9},{5,13},{9,1},{13,5},{2,10},{6,14},... | collective-permute-start | bytes 2752520 | tf_op jit(solution)/shard_map/ppermute | solution.py:178
  164.7 23.6 %collective-permute-start.12 = (bf16[64,7168]{1,0:T(8,128)(2,1)S(1)}, bf16[64,7168]{1,0:T(8,128)(2,1)S(1)}, u32[]{:S(2)}, u32[]{:S(2)}) collective-permute-start(bf16[64,7168]{1,0:T(8,128)(2,1)S(1)} %activate.4.refs_2_.refs_0_), channel_id=1, source_target_pairs={{0,4},{4,0},{8,12},{12,8},{1,5},{5,1},{9,13},{13,9},{2,6},{6,2},{1... | collective-permute-start | bytes 2752520 | tf_op jit(solution)/shard_map/ppermute | solution.py:178
  185.8 2.5 collective-permute-start.14
  186.7 22.8 %collective-permute-start.18 = (bf16[2,32,7168]{2,1,0:T(8,128)(2,1)S(1)}, bf16[2,32,7168]{2,1,0:T(8,128)(2,1)S(1)}, u32[]{:S(2)}, u32[]{:S(2)}) collective-permute-start(bf16[2,32,7168]{2,1,0:T(8,128)(2,1)S(1)} %get-tuple-element.37.refs_5_), channel_id=1, source_target_pairs={{0,8},{4,12},{8,0},{12,4},{1,9},{5,13},{9,1},{13,5},{2,10},{6,14},... | collective-permute-start | bytes 2752520 | tf_op jit(solution)/shard_map/ppermute | solution.py:178
  207.7 15.9 %collective-permute-start.16 = (bf16[128,2048]{1,0:T(8,128)(2,1)S(1)}, bf16[128,2048]{1,0:T(8,128)(2,1)S(1)}, u32[]{:S(2)}, u32[]{:S(2)}) collective-permute-start(bf16[128,2048]{1,0:T(8,128)(2,1)S(1)} %get-tuple-element.38.refs_2_), channel_id=1, source_target_pairs={{0,1},{1,2},{2,3},{3,0},{4,5},{5,6},{6,7},{7,4},{8,9},{9,10},{10,1... | collective-permute-start | bytes 1572872 | tf_op jit(solution)/shard_map/ppermute | solution.py:175
  210.2 12.2 %collective-permute-start.20 = (bf16[32,7168]{1,0:T(8,128)(2,1)S(1)}, bf16[32,7168]{1,0:T(8,128)(2,1)S(1)}, u32[]{:S(2)}, u32[]{:S(2)}) collective-permute-start(bf16[32,7168]{1,0:T(8,128)(2,1)S(1)} %activate.5.refs_0_.refs_5_), channel_id=1, source_target_pairs={{0,8},{4,12},{8,0},{12,4},{1,9},{5,13},{9,1},{13,5},{2,10},{6,14},... | collective-permute-start | bytes 1376264 | tf_op jit(solution)/shard_map/ppermute | solution.py:178
  211.7 12.0 %collective-permute-start.19 = (bf16[32,7168]{1,0:T(8,128)(2,1)S(1)}, bf16[32,7168]{1,0:T(8,128)(2,1)S(1)}, u32[]{:S(2)}, u32[]{:S(2)}) collective-permute-start(bf16[32,7168]{1,0:T(8,128)(2,1)S(1)} %activate.5.refs_0_.refs_5_), channel_id=1, source_target_pairs={{0,4},{4,0},{8,12},{12,8},{1,5},{5,1},{9,13},{13,9},{2,6},{6,2},{1... | collective-permute-start | bytes 1376264 | tf_op jit(solution)/shard_map/ppermute | solution.py:178
  222.4 1.8 collective-permute-start.21
  223.7 33.3 %copy-start.1 = (bf16[128,2048]{1,0:T(8,128)(2,1)S(1)}, bf16[128,2048]{1,0:T(8,128)(2,1)}, u32[]{:S(2)}) copy-start(bf16[128,2048]{1,0:T(8,128)(2,1)} %refs_0_.3) | copy-start | bytes 1572868
  223.7 17.4 %collective-permute-start.17 = (bf16[128,2048]{1,0:T(8,128)(2,1)S(1)}, bf16[128,2048]{1,0:T(8,128)(2,1)S(1)}, u32[]{:S(2)}, u32[]{:S(2)}) collective-permute-start(bf16[128,2048]{1,0:T(8,128)(2,1)S(1)} %add_convert_fusion.2), channel_id=1, source_target_pairs={{0,1},{1,2},{2,3},{3,0},{4,5},{5,6},{6,7},{7,4},{8,9},{9,10},{10,1... | collective-permute-start | bytes 1572872 | tf_op jit(solution)/shard_map/ppermute | solution.py:175
  241.2 15.8 %collective-permute-start.22 = (bf16[128,2048]{1,0:T(8,128)(2,1)S(1)}, bf16[128,2048]{1,0:T(8,128)(2,1)S(1)}, u32[]{:S(2)}, u32[]{:S(2)}) collective-permute-start(bf16[128,2048]{1,0:T(8,128)(2,1)S(1)} %add_convert_fusion.1), channel_id=1, source_target_pairs={{0,1},{1,2},{2,3},{3,0},{4,5},{5,6},{6,7},{7,4},{8,9},{9,10},{10,1... | collective-permute-start | bytes 1572872 | tf_op jit(solution)/shard_map/ppermute | solution.py:175
where the time goes:
time: 259 us; the launch traced here: 258 us
  Pallas kernels  143 us (55%)
  waiting for transfers between devices  96.2 us (37%)
  starting transfers between devices  14.6 us (6%)
  local copies, waits for them, and re-layouts  3.12 us (1%)
    pallas_call x4, Pallas kernels, first_dots(): pl.pallas_call(kernel, grid=(width // step,), in_specs=[pl.BlockSpec((row...  83.6 us
    ppermute x17, waiting for transfers between devices, swap(): lax.ppermute(value, 'pipe', [(i, i ^ 1 << bit) for i in range(n_pipe)])  66.2 us
    pallas_call x3, Pallas kernels, last_dot(): pl.pallas_call(kernel, grid=(depth // step,), in_specs=[pl.BlockSpec((m1,...  53.1 us
    ppermute x6, waiting for transfers between devices, hop(): return lax.ppermute(value, 'tensor', ring)  30 us
    ppermute x17, starting transfers between devices, swap(): lax.ppermute(value, 'pipe', [(i, i ^ 1 << bit) for i in range(n_pipe)])  9.78 us
  transfers between devices with their start and end apart: 23, of which 11 were waited for; matrix products, arithmetic and copies ran while one was open for 0% of the time, Pallas kernels for 44%

commit v1 on v0

v1 whole, which is shorter than its diff:
```python
import jax
import jax.numpy as jnp
from jax import lax
from jax.experimental import pallas as pl
from jax.experimental.pallas import tpu as pltpu
from jax.sharding import PartitionSpec as P

BF16, F32 = jnp.bfloat16, jnp.float32
MIB = 1 << 20
ANY = pl.BlockSpec(memory_space=pl.ANY)
HBM = pl.BlockSpec(memory_space=pltpu.HBM)


def block_of(size, most):
    return max(b for b in range(128, most + 1, 128) if size % b == 0)


def params(mib):
    return pltpu.CompilerParams(vmem_limit_bytes=mib * MIB, dimension_semantics=("arbitrary",))


def cost(flops, moved, exps=0):
    return pl.CostEstimate(flops=flops, bytes_accessed=moved, transcendentals=exps)


def cut_order(bits):
    order = [0]
    for bit in reversed(range(bits)):
        order = order + [j | 1 << bit for j in order]
    return order


def first_dots(shards, weights, columns, bits, after):
    rows, depth = shards[0].shape
    at, width = columns
    n, g, k = 1 << bits, len(shards), len(weights)
    r, m = rows // n, len(shards) * rows
    step = block_of(width, 512)
    steps = width // step
    slots = min(4, steps)
    order = cut_order(bits)

    def kernel(*refs):
        x, w = refs[:g], refs[g : g + k]
        keep, send, held, buf, x_sem, w_sem = refs[-6:]
        c = pl.program_id(0)

        def load(i, block):
            slot = block % slots
            start = pl.multiple_of(at + block * step, 128)
            return pltpu.make_async_copy(w[i].at[:, pl.ds(start, step)], buf.at[i, slot], w_sem.at[i, slot])

        @pl.when(c == 0)
        def _():
            for block in range(slots):
                for i in range(k):
                    load(i, block).start()
            me = lax.axis_index("pipe")
            copies = []
            for spot, j in enumerate(order):
                start = pl.multiple_of((me ^ j) * r, r)
                for i in range(g):
                    to = spot * g + i
                    copies.append(
                        pltpu.make_async_copy(
                            x[i].at[pl.ds(start, r), :], held.at[pl.ds(to * r, r), :], x_sem.at[to]
                        )
                    )
            for copy in copies:
                copy.start()
            for copy in copies:
                copy.wait()

        for i in range(k):
            load(i, c).wait()
            part = jnp.dot(held[...], buf[i, c % slots], preferred_element_type=F32).astype(BF16)
            keep[i] = part[: m // 2]
            send[i] = part[m // 2 :]

        @pl.when(c + slots < steps)
        def _():
            for i in range(k):
                load(i, c + slots).start()

    out = jax.ShapeDtypeStruct((k, m // 2, width), BF16)
    return pl.pallas_call(
        kernel,
        grid=(steps,),
        in_specs=[ANY] * (g + k + len(after)),
        out_specs=[pl.BlockSpec((k, m // 2, step), lambda c: (0, 0, c))] * 2,
        out_shape=[out, out],
        scratch_shapes=[
            pltpu.VMEM((m, depth), BF16),
            pltpu.VMEM((k, slots, depth, step), BF16),
            pltpu.SemaphoreType.DMA((n * g,)),
            pltpu.SemaphoreType.DMA((k, slots)),
        ],
        compiler_params=params(40),
        cost_estimate=cost(2 * k * m * depth * width, 2 * k * depth * width),
        name="first_dots",
    )(*shards, *weights, *after)


def partner_of(got, k, bit):
    if bit == 0:
        return [got[i] for i in range(k)]
    other = 1 - ((lax.axis_index("pipe") >> bit) & 1)
    return [got[other * k + i] for i in range(k)]


def fold(keep, got, bit, after):
    k, m, width = keep.shape
    step = block_of(width, 1024)

    def kernel(*refs):
        a, b = refs[:2]
        stay, send = refs[-2:]
        for i, other in enumerate(partner_of(b, k, bit)):
            total = (a[i].astype(F32) + other.astype(F32)).astype(BF16)
            stay[i] = total[: m // 2]
            send[i] = total[m // 2 :]

    out = jax.ShapeDtypeStruct((k, m // 2, width), BF16)
    return pl.pallas_call(
        kernel,
        grid=(width // step,),
        in_specs=[pl.BlockSpec((a.shape[0], m, step), lambda c: (0, 0, c)) for a in (keep, got)]
        + [ANY] * len(after),
        out_specs=[pl.BlockSpec((k, m // 2, step), lambda c: (0, 0, c))] * 2,
        out_shape=[out, out],
        compiler_params=params(24),
        cost_estimate=cost(k * m * width, 6 * k * m * width),
        name="fold",
    )(keep, got, *after)


def activate(pairs, bit, after):
    m = pairs[0][0].shape[1]
    widths = [a.shape[2] for a, _ in pairs]
    flat = [a for pair in pairs for a in pair]

    def kernel(*refs):
        out = refs[-1]
        at = 0
        for i, width in enumerate(widths):
            a, b = refs[2 * i], refs[2 * i + 1]
            gate_got, up_got = partner_of(b, 2, bit)
            gate = a[0].astype(F32) + gate_got.astype(F32)
            up = a[1].astype(F32) + up_got.astype(F32)
            out[0, :, at : at + width] = (gate / (1.0 + jnp.exp(-gate)) * up).astype(BF16)
            at += width

    return pl.pallas_call(
        kernel,
        in_specs=[pl.BlockSpec(memory_space=pltpu.VMEM)] * len(flat) + [ANY] * len(after),
        out_specs=pl.BlockSpec(memory_space=pltpu.VMEM),
        out_shape=jax.ShapeDtypeStruct((1, m, sum(widths)), BF16),
        compiler_params=pltpu.CompilerParams(vmem_limit_bytes=24 * MIB),
        cost_estimate=cost(8 * m * sum(widths), 10 * m * sum(widths), m * sum(widths)),
        name="activate",
    )(*flat, *after)


def last_dot(own, other, weight, at, g, carry, final, after):
    half, m1, depth = own.shape
    width = weight.shape[1]
    r, m = m1 // g, 2 * half * m1
    step = block_of(depth, 512)
    steps = depth // step
    slots = min(4, steps)
    given = [own, other, weight] + ([] if carry is None else [carry])

    def kernel(*refs):
        h, w = refs[:2], refs[2]
        n_out = g if final else 1
        outs = refs[-5 - n_out : -5]
        total, rows, buf, h_sem, w_sem = refs[-5:]
        c = pl.program_id(0)

        def load(block):
            slot = block % slots
            start = pl.multiple_of(at + block * step, 128)
            return pltpu.make_async_copy(w.at[pl.ds(start, step), :], buf.at[slot], w_sem.at[slot])

        @pl.when(c == 0)
        def _():
            for block in range(slots):
                load(block).start()
            copies = [pltpu.make_async_copy(h[i], rows.at[pl.ds(i * half, half)], h_sem.at[i]) for i in range(2)]
            if carry is not None:
                copies.append(pltpu.make_async_copy(refs[3], total, h_sem.at[2]))
            for copy in copies:
                copy.start()
            if carry is None:
                total[...] = jnp.zeros_like(total)
            for copy in copies:
                copy.wait()

        load(c).wait()
        start = pl.multiple_of(c * step, 128)
        part = rows[:, :, pl.ds(start, step)].reshape(m, step)
        total[...] += jnp.dot(part, buf[c % slots], preferred_element_type=F32)

        @pl.when(c + slots < steps)
        def _():
            load(c + slots).start()

        @pl.when(c == steps - 1)
        def _():
            if not final:
                outs[0][...] = total[...]
                return
            core = lax.axis_index("pipe") & 1
            for q in range(2 * half):
                block = 2 * q + core if q < half else 2 * (q - half) + 1 - core
                start = pl.multiple_of(block * r, r)
                for i in range(g):
                    spot = (q * g + i) * r
                    outs[i][pl.ds(start, r), :] = total[spot : spot + r, :].astype(BF16)

    if final:
        shapes = [jax.ShapeDtypeStruct((m // g, width), BF16)] * g
    else:
        shapes = [jax.ShapeDtypeStruct((m, width), F32)]
    return pl.pallas_call(
        kernel,
        grid=(steps,),
        in_specs=[HBM] * 3 + [ANY] * (len(given) - 3 + len(after)),
        out_specs=[pl.BlockSpec(s.shape, lambda c: (0, 0)) for s in shapes],
        out_shape=shapes,
        scratch_shapes=[
            pltpu.VMEM((m, width), F32),
            pltpu.VMEM((2 * half, m1, depth), BF16),
            pltpu.VMEM((slots, step, width), BF16),
            pltpu.SemaphoreType.DMA((3,)),
            pltpu.SemaphoreType.DMA((slots,)),
        ],
        compiler_params=params(40),
        cost_estimate=cost(2 * m * depth * width, 2 * depth * width),
        name="last_dot",
    )(*given, *after)


def pieces_of(width, count):
    block = block_of(width, 512)
    blocks = width // block
    count = min(count, blocks)
    ends = [blocks * i // count * block for i in range(count + 1)]
    return [(a, b - a) for a, b in zip(ends, ends[1:])]


def solution(mesh):
    n_pipe, n_tensor = mesh.shape["pipe"], mesh.shape["tensor"]
    bits = n_pipe.bit_length() - 1
    assert n_pipe == 1 << bits and bits >= 2 and n_tensor >= 3
    ring = [(i, (i + 1) % n_tensor) for i in range(n_tensor)]
    pairs_of = [[[i, i | 1 << bit] for i in range(n_pipe) if not i >> bit & 1] for bit in range(bits)]

    def hop(value):
        return lax.ppermute(value, "tensor", ring)

    def swap_core(value):
        return lax.ppermute(value, "pipe", [(i, i ^ 1) for i in range(n_pipe)])

    def exchange(value, bit):
        return lax.all_gather(value, "pipe", axis=0, tiled=True, axis_index_groups=pairs_of[bit])

    middle = list(range(1, n_tensor - 1))
    chunks = [[0]] + [middle[i : i + 2] for i in range(0, len(middle), 2)] + [[n_tensor - 1]]

    def shards(tokens, gate_weight, up_weight, down_weight):
        width = gate_weight.shape[1]
        held = [tokens]
        for _ in range(n_tensor - 1):
            held.append(hop(held[-1]))
        last = []

        cuts, groups = [], []
        for i, chunk in enumerate(chunks):
            cuts.append(pieces_of(width, 2 if i == len(chunks) - 1 else 4))
            n = len(cuts[i])
            groups.append([list(range(n))] if i == 0 else [list(range((n + 1) // 2)), list(range((n + 1) // 2, n))])
        items = [(i, p) for i in range(len(chunks)) for p in range(len(cuts[i]))]
        dotted, folded, hidden = {}, {}, {}

        def dots(i, p):
            keep, send = first_dots(
                [held[s] for s in chunks[i]], [gate_weight, up_weight], cuts[i][p], bits, last
            )
            last[:] = [send]
            dotted[i, p] = keep, swap_core(send)

        def folds(i, p):
            keep, got = dotted[i, p]
            for bit in range(bits - 1):
                keep, send = fold(keep, got, bit, last)
                last[:] = [send]
                got = exchange(send, bit + 1)
            folded[i, p] = keep, got

        def act(i, q):
            own = activate([folded[i, p] for p in groups[i][q]], bits - 1, last)
            last[:] = [own]
            for bit in range(1, bits):
                own = exchange(own, bit)
            hidden[i, q] = own, swap_core(own)

        sums, terms = {}, {}

        def down(i, q):
            final = q == len(groups[i]) - 1
            own, other = hidden[i, q]
            out = last_dot(
                own, other, down_weight, cuts[i][groups[i][q][0]][0], len(chunks[i]), sums.get(i), final, last
            )
            last[:] = out[:1]
            if final:
                terms.update(zip(chunks[i], out))
            else:
                sums[i] = out[0]

        todo = [(i, q, items.index((i, groups[i][q][-1]))) for i in range(len(chunks)) for q in range(len(groups[i]))]
        for k, item in enumerate(items):
            dots(*item)
            if k:
                folds(*items[k - 1])
            while todo and todo[0][2] <= k - 3 and todo[0][0] < len(chunks) - 1:
                act(*todo.pop(0)[:2])
        down(0, 0)
        end = len(chunks) - 1
        while todo[0][0] < end:
            act(*todo.pop(0)[:2])
        folds(*items[-1])
        for i in range(1, end):
            down(i, 0)
            if i == end - 1:
                act(end, 0)
            down(i, 1)
        act(end, 1)
        down(end, 0)
        down(end, 1)

        total = terms[1].astype(F32)
        for i in list(range(2, n_tensor)) + [0]:
            total = hop(total.astype(BF16)).astype(F32) + terms[i].astype(F32)
        return (tokens.astype(F32) + total).astype(BF16)

    return jax.shard_map(
        shards,
        mesh=mesh,
        in_specs=(
            P(("dp", "tensor"), "pipe"),
            P("pipe", "tensor"),
            P("pipe", "tensor"),
            P("tensor", "pipe"),
        ),
        out_specs=P(("dp", "tensor"), "pipe"),
        check_vma=False,
    )
```

time: 259 us -> 340 us (1.31)
  blocking collectives: 0 us -> 145 us
  waiting for transfers between devices: 96.2 us -> 20 us
  local copies, waits for them, and re-layouts: 3.12 us -> 22.2 us
  Pallas kernels: 143 us -> 128 us
  between operations: 0.21 us -> 14 us
  starting transfers between devices: 14.6 us -> 8.91 us
    all_gather x0 -> x13, blocking collectives: none -> 145 us  [exchange(): lax.all_gather(value, 'pipe', axis=0, tiled=True, axis_index_groups=pairs...]
    ppermute x17 -> x15, waiting for transfers between devices: 66.2 us -> 0.04 us  [swap_core(): return lax.ppermute(value, 'pipe', [(i, i ^ 1) for i in range(n_pipe)])]
    unnamed x6 -> x74, local copies, waits for them, and re-layouts: 3.12 us -> 22.2 us
    pallas_call x14 -> x30, Pallas kernels: 143 us -> 128 us  [the longest x10 75.8 us: first_dots(): pl.pallas_call(kernel, grid=(steps,), in_specs=[ANY] * (g + k + len(after...]
    ppermute x6, waiting for transfers between devices: 30 us -> 19.9 us  [hop(): return lax.ppermute(value, 'tensor', ring)]
    ppermute x17 -> x15, starting transfers between devices: 9.78 us -> 3.04 us  [swap_core(): return lax.ppermute(value, 'pipe', [(i, i ^ 1) for i in range(n_pipe)])]
  transfers between devices with their start and end apart: 23 -> 23, of which waited for: 11 -> 4; matrix products, arithmetic and copies ran while one was open for 0% -> 0% of each run, Pallas kernels for 44% -> 36%
where the time goes in v1:
time: 340 us; the launch traced here: 339 us
  blocking collectives  145 us (43%)
  Pallas kernels  128 us (38%)
  local copies, waits for them, and re-layouts  22.2 us (7%)
  waiting for transfers between devices  20 us (6%)
  between operations  14 us (4%)
  starting transfers between devices  8.91 us (3%)
    all_gather x13, blocking collectives, exchange(): lax.all_gather(value, 'pipe', axis=0, tiled=True, axis_index_groups=pairs...  145 us
    pallas_call x10, Pallas kernels, first_dots(): pl.pallas_call(kernel, grid=(steps,), in_specs=[ANY] * (g + k + len(after...  75.8 us
    pallas_call x5, Pallas kernels, last_dot(): pl.pallas_call(kernel, grid=(steps,), in_specs=[HBM] * 3 + [ANY] * (len(g...  39.7 us
    unnamed x74, local copies, waits for them, and re-layouts  22.2 us
    ppermute x6, waiting for transfers between devices, hop(): return lax.ppermute(value, 'tensor', ring)  19.9 us
    pallas_call x10, Pallas kernels, fold(): pl.pallas_call(kernel, grid=(width // step,), in_specs=[pl.BlockSpec((a.s...  10.4 us
  transfers between devices with their start and end apart: 23, of which 4 were waited for; matrix products, arithmetic and copies ran while one was open for 0% of the time, Pallas kernels for 36%

profile of v1, /device:TPU:0, one launch (start us, length us, event | category | flops | bytes accessed | tf_op | source)
XLA Modules:
  0.0 339.2 jit_solution(13131881230118623334)
XLA Ops:
  6.5 3.0 collective-permute-start
  9.6 1.1 copy-done
  10.6 5.3 %first_dots.10 = (bf16[2,64,1536]{2,1,0:T(8,128)(2,1)S(1)}, bf16[2,64,1536]{2,1,0:T(8,128)(2,1)S(1)}) custom-call(bf16[128,2048]{1,0:T(8,128)(2,1)S(1)} %copy-done, bf16[2048,7168]{1,0:T(8,128)(2,1)} %refs_1_.11, bf16[2048,7168]{1,0:T(8,128)(2,1)} %refs_2_.24), custom_call_target="tpu_custom_call" | custom-call | flops 1610612736 | bytes 12582912 | tf_op jit(solution)/shard_map/first_dots/pallas_call | solution.py:86
  16.0 6.5 %first_dots.11 = (bf16[2,64,2048]{2,1,0:T(8,128)(2,1)S(1)}, bf16[2,64,2048]{2,1,0:T(8,128)(2,1)S(1)}) custom-call(bf16[128,2048]{1,0:T(8,128)(2,1)S(1)} %copy-done, bf16[2048,7168]{1,0:T(8,128)(2,1)} %refs_1_.11, bf16[2048,7168]{1,0:T(8,128)(2,1)} %refs_2_.24, bf16[2,64,1536]{2,1,0:T(8,128)(2,1)S(1)} %get-tuple-element.48.refs_3_), custom_call_target="tpu_custom_call" | custom-call | flops 2147483648 | bytes 16777216 | tf_op jit(solution)/shard_map/first_dots/pallas_call | solution.py:86
  22.6 0.6 collective-permute-start.4
  23.7 1.3 collective-permute-start.1
  25.0 5.3 %first_dots.12 = (bf16[2,64,1536]{2,1,0:T(8,128)(2,1)S(1)}, bf16[2,64,1536]{2,1,0:T(8,128)(2,1)S(1)}) custom-call(bf16[128,2048]{1,0:T(8,128)(2,1)S(1)} %copy-done, bf16[2048,7168]{1,0:T(8,128)(2,1)} %refs_1_.11, bf16[2048,7168]{1,0:T(8,128)(2,1)} %refs_2_.24, bf16[2,32,1536]{2,1,0:T(8,128)(2,1)S(1)} %get-tuple-element.50.refs_3_), custom_call_target="tpu_custom_call" | custom-call | flops 1610612736 | bytes 12582912 | tf_op jit(solution)/shard_map/first_dots/pallas_call | solution.py:86
  30.7 6.6 %first_dots.13 = (bf16[2,64,2048]{2,1,0:T(8,128)(2,1)S(1)}, bf16[2,64,2048]{2,1,0:T(8,128)(2,1)S(1)}) custom-call(bf16[128,2048]{1,0:T(8,128)(2,1)S(1)} %copy-done, bf16[2048,7168]{1,0:T(8,128)(2,1)} %refs_1_.11, bf16[2048,7168]{1,0:T(8,128)(2,1)} %refs_2_.24, bf16[2,32,2048]{2,1,0:T(8,128)(2,1)S(1)} %get-tuple-element.54.refs_3_), custom_call_target="tpu_custom_call" | custom-call | flops 2147483648 | bytes 16777216 | tf_op jit(solution)/shard_map/first_dots/pallas_call | solution.py:86
  38.2 0.7 copy-done.35
  39.1 6.1 %first_dots.14 = (bf16[2,128,1536]{2,1,0:T(8,128)(2,1)S(1)}, bf16[2,128,1536]{2,1,0:T(8,128)(2,1)S(1)}) custom-call(bf16[128,2048]{1,0:T(8,128)(2,1)S(1)} %collective-permute-done.refs_0_, bf16[128,2048]{1,0:T(8,128)(2,1)S(1)} %collective-permute-done.1.refs_1_, bf16[2048,7168]{1,0:T(8,128)(2,1)} %refs_1_.11, bf16[2048,7168]{1,0:T(8,128)(2,1)} %refs_2_.24, ...), custom_call_target="tpu_custom_call" | custom-call | flops 3221225472 | bytes 12582912 | tf_op jit(solution)/shard_map/first_dots/pallas_call | solution.py:86
  45.6 0.7 copy-done.31
  46.3 7.5 %first_dots.15 = (bf16[2,128,2048]{2,1,0:T(8,128)(2,1)S(1)}, bf16[2,128,2048]{2,1,0:T(8,128)(2,1)S(1)}) custom-call(bf16[128,2048]{1,0:T(8,128)(2,1)S(1)} %collective-permute-done.refs_0_, bf16[128,2048]{1,0:T(8,128)(2,1)S(1)} %collective-permute-done.1.refs_1_, bf16[2048,7168]{1,0:T(8,128)(2,1)} %refs_1_.11, bf16[2048,7168]{1,0:T(8,128)(2,1)} %refs_2_.24, ...), custom_call_target="tpu_custom_call" | custom-call | flops 4294967296 | bytes 16777216 | tf_op jit(solution)/shard_map/first_dots/pallas_call | solution.py:86
  54.4 7.6 %all_gather.45.refs_1_ = bf16[4,32,1536]{2,1,0:T(8,128)(2,1)} all-gather(bf16[2,32,1536]{2,1,0:T(8,128)(2,1)S(1)} %get-tuple-element.50.refs_3_), channel_id=1, replica_groups={{0,8},{4,12},{1,9},{5,13},{2,10},{6,14},{3,11},{7,15},{16,24},{20,28},{..., dimensions={0}, use_global_device_ids=true | all-gather | bytes 589824 | tf_op jit(solution)/shard_map/all_gather | solution.py:266
  62.0 8.1 %all_gather.46.refs_3_ = bf16[4,32,2048]{2,1,0:T(8,128)(2,1)S(1)} all-gather(bf16[2,32,2048]{2,1,0:T(8,128)(2,1)S(1)} %get-tuple-element.54.refs_3_), channel_id=1, replica_groups={{0,8},{4,12},{1,9},{5,13},{2,10},{6,14},{3,11},{7,15},{16,24},{20,28},{..., dimensions={0}, use_global_device_ids=true | all-gather | bytes 786432 | tf_op jit(solution)/shard_map/all_gather | solution.py:266
  70.1 6.4 %all_gather.47.refs_5_ = bf16[4,32,1536]{2,1,0:T(8,128)(2,1)} all-gather(bf16[2,32,1536]{2,1,0:T(8,128)(2,1)S(1)} %get-tuple-element.56.refs_4_), channel_id=1, replica_groups={{0,8},{4,12},{1,9},{5,13},{2,10},{6,14},{3,11},{7,15},{16,24},{20,28},{..., dimensions={0}, use_global_device_ids=true | all-gather | bytes 589824 | tf_op jit(solution)/shard_map/all_gather | solution.py:266
  76.5 1.3 collective-permute-start.10
  77.9 7.0 %all_gather.48.refs_7_ = bf16[4,32,2048]{2,1,0:T(8,128)(2,1)S(1)} all-gather(bf16[2,32,2048]{2,1,0:T(8,128)(2,1)S(1)} %get-tuple-element.60.refs_4_), channel_id=1, replica_groups={{0,8},{4,12},{1,9},{5,13},{2,10},{6,14},{3,11},{7,15},{16,24},{20,28},{..., dimensions={0}, use_global_device_ids=true | all-gather | bytes 786432 | tf_op jit(solution)/shard_map/all_gather | solution.py:266
  85.3 7.1 %first_dots.16 = (bf16[2,128,1536]{2,1,0:T(8,128)(2,1)S(1)}, bf16[2,128,1536]{2,1,0:T(8,128)(2,1)}) custom-call(bf16[128,2048]{1,0:T(8,128)(2,1)S(1)} %collective-permute-done.refs_0_, bf16[128,2048]{1,0:T(8,128)(2,1)S(1)} %collective-permute-done.1.refs_1_, bf16[2048,7168]{1,0:T(8,128)(2,1)} %refs_1_.11, bf16[2048,7168]{1,0:T(8,128)(2,1)} %refs_2_.24, ...), custom_call_target="tpu_custom_call" | custom-call | flops 3221225472 | bytes 12582912 | tf_op jit(solution)/shard_map/first_dots/pallas_call | solution.py:86
  92.5 1.2 fold.15
  93.7 0.8 copy-done.19
  94.5 1.0 copy-done.8
  95.5 0.9 copy-done.30
  96.5 0.9 copy-done.32
  97.4 0.9 copy-done.34
  98.4 0.9 copy-done.36
  99.7 8.3 %first_dots.17 = (bf16[2,128,2048]{2,1,0:T(8,128)(2,1)S(1)}, bf16[2,128,2048]{2,1,0:T(8,128)(2,1)}) custom-call(bf16[128,2048]{1,0:T(8,128)(2,1)S(1)} %collective-permute-done.refs_0_, bf16[128,2048]{1,0:T(8,128)(2,1)S(1)} %collective-permute-done.1.refs_1_, bf16[2048,7168]{1,0:T(8,128)(2,1)} %refs_1_.11, bf16[2048,7168]{1,0:T(8,128)(2,1)} %refs_2_.24, ...), custom_call_target="tpu_custom_call" | custom-call | flops 4294967296 | bytes 16777216 | tf_op jit(solution)/shard_map/first_dots/pallas_call | solution.py:86
  108.6 17.2 %all_gather.51.refs_0_ = bf16[2,32,7168]{2,1,0:T(8,128)(2,1)S(1)} all-gather(bf16[1,32,7168]{2,1,0:T(8,128)(2,1)S(1)} %activate.5.refs_4_), channel_id=1, replica_groups={{0,8},{4,12},{1,9},{5,13},{2,10},{6,14},{3,11},{7,15},{16,24},{20,28},{..., dimensions={0}, use_global_device_ids=true | all-gather | bytes 1376256 | tf_op jit(solution)/shard_map/all_gather | solution.py:266
  125.8 1.1 copy-done.18
  126.9 1.3 fold.16
  128.2 0.7 copy-done.27
  129.0 11.6 %first_dots.18 = (bf16[2,64,3584]{2,1,0:T(8,128)(2,1)S(1)}, bf16[2,64,3584]{2,1,0:T(8,128)(2,1)}) custom-call(bf16[128,2048]{1,0:T(8,128)(2,1)S(1)} %collective-permute-done.10.refs_0_, bf16[2048,7168]{1,0:T(8,128)(2,1)} %refs_1_.11, bf16[2048,7168]{1,0:T(8,128)(2,1)} %refs_2_.24, bf16[2,64,1536]{2,1,0:T(8,128)(2,1)S(1)} %get-tuple-element.73.refs_3_), custom_call_target="tpu_custom_call" | custom-call | flops 3758096384 | bytes 29360128 | tf_op jit(solution)/shard_map/first_dots/pallas_call | solution.py:86
  140.6 0.6 collective-permute-start.12
  141.2 12.5 %all_gather.52.refs_1_ = bf16[4,64,1536]{2,1,0:T(8,128)(2,1)S(1)} all-gather(bf16[2,64,1536]{2,1,0:T(8,128)(2,1)S(1)} %copy-done.6), channel_id=1, replica_groups={{0,8},{4,12},{1,9},{5,13},{2,10},{6,14},{3,11},{7,15},{16,24},{20,28},{..., dimensions={0}, use_global_device_ids=true | all-gather | bytes 1179648 | tf_op jit(solution)/shard_map/all_gather | solution.py:266
  153.6 1.2 copy-done.12
  154.8 2.1 fold.17
  156.9 0.8 copy-done.21
  157.8 15.2 %all_gather.49.refs_1_ = bf16[4,64,1536]{2,1,0:T(8,128)(2,1)S(1)} all-gather(bf16[2,64,1536]{2,1,0:T(8,128)(2,1)S(1)} %get-tuple-element.73.refs_3_), channel_id=1, replica_groups={{0,8},{4,12},{1,9},{5,13},{2,10},{6,14},{3,11},{7,15},{16,24},{20,28},{..., dimensions={0}, use_global_device_ids=true | all-gather | bytes 1179648 | tf_op jit(solution)/shard_map/all_gather | solution.py:266
  173.0 1.2 copy-done.9
  174.2 1.0 copy-done.26
  175.6 1.0 copy-done.3
  176.7 11.4 %first_dots.19 = (bf16[2,64,3584]{2,1,0:T(8,128)(2,1)S(1)}, bf16[2,64,3584]{2,1,0:T(8,128)(2,1)}) custom-call(bf16[128,2048]{1,0:T(8,128)(2,1)S(1)} %copy-done.3, bf16[2048,7168]{1,0:T(8,128)(2,1)} %refs_1_.11, bf16[2048,7168]{1,0:T(8,128)(2,1)} %refs_2_.24, bf16[1,64,3584]{2,1,0:T(8,128)(2,1)S(1)} %activate.6.refs_3_), custom_call_target="tpu_custom_call" | custom-call | flops 3758096384 | bytes 29360128 | tf_op jit(solution)/shard_map/first_dots/pallas_call | solution.py:86
  188.1 0.9 copy-done.13
  189.1 14.3 %all_gather.55.refs_0_ = bf16[2,64,3584]{2,1,0:T(8,128)(2,1)S(1)} all-gather(bf16[1,64,3584]{2,1,0:T(8,128)(2,1)S(1)} %activate.6.refs_3_), channel_id=1, replica_groups={{0,8},{4,12},{1,9},{5,13},{2,10},{6,14},{3,11},{7,15},{16,24},{20,28},{..., dimensions={0}, use_global_device_ids=true | all-gather | bytes 1376256 | tf_op jit(solution)/shard_map/all_gather | solution.py:266
  203.4 2.2 fold.18
  205.7 0.8 copy-done.23
  206.4 11.8 %last_dot.5.refs_4_ = bf16[128,2048]{1,0:T(8,128)(2,1)S(1)} custom-call(bf16[2,32,7168]{2,1,0:T(8,128)(2,1)S(1)} %all_gather.51.refs_0_, bf16[2,32,7168]{2,1,0:T(8,128)(2,1)} %collective-permute-done.11.refs_1_, bf16[7168,2048]{1,0:T(8,128)(2,1)} %refs_2_.29, bf16[2,32,3584]{2,1,0:T(8,128)(2,1)S(1)} %get-tuple-element.82.refs_3_), custom_call_target="tpu_custom_call" | custom-call | flops 3758096384 | bytes 29360128 | tf_op jit(solution)/shard_map/last_dot/pallas_call | solution.py:225
  218.3 0.8 copy-done.4
  219.1 1.2 copy-done.10
  220.3 1.0 copy-done.22
  221.8 13.6 %all_gather.54.refs_0_ = bf16[2,64,3584]{2,1,0:T(8,128)(2,1)S(1)} all-gather(bf16[1,64,3584]{2,1,0:T(8,128)(2,1)S(1)} %activate.7.refs_2_), channel_id=1, replica_groups={{0,8},{4,12},{1,9},{5,13},{2,10},{6,14},{3,11},{7,15},{16,24},{20,28},{..., dimensions={0}, use_global_device_ids=true | all-gather | bytes 1376256 | tf_op jit(solution)/shard_map/all_gather | solution.py:266
  235.4 13.8 %all_gather.56.refs_1_ = bf16[4,32,3584]{2,1,0:T(8,128)(2,1)S(1)} all-gather(bf16[2,32,3584]{2,1,0:T(8,128)(2,1)} %copy-done.4), channel_id=1, replica_groups={{0,8},{4,12},{1,9},{5,13},{2,10},{6,14},{3,11},{7,15},{16,24},{20,28},{..., dimensions={0}, use_global_device_ids=true | all-gather | bytes 1376256 | tf_op jit(solution)/shard_map/all_gather | solution.py:266
  249.2 1.2 copy-done.14
  250.4 2.2 fold.19
  252.6 9.0 %last_dot.6.refs_2_.refs_3_ = f32[256,2048]{1,0:T(8,128)S(1)} custom-call(bf16[2,64,3584]{2,1,0:T(8,128)(2,1)S(1)} %all_gather.55.refs_0_, bf16[2,64,3584]{2,1,0:T(8,128)(2,1)} %collective-permute-done.14.refs_1_, bf16[7168,2048]{1,0:T(8,128)(2,1)} %refs_2_.29, bf16[2,32,3584]{2,1,0:T(8,128)(2,1)S(1)} %get-tuple-element.84.refs_3_), custom_call_target="tpu_custom_call" | custom-call | flops 3758096384 | bytes 14680064 | tf_op jit(solution)/shard_map/last_dot/pallas_call | solution.py:225
  261.6 1.0 copy-done.24
  262.9 6.8 %last_dot.7 = (bf16[128,2048]{1,0:T(8,128)(2,1)S(1)}, bf16[128,2048]{1,0:T(8,128)(2,1)S(1)}) custom-call(bf16[2,64,3584]{2,1,0:T(8,128)(2,1)S(1)} %all_gather.54.refs_0_, bf16[2,64,3584]{2,1,0:T(8,128)(2,1)S(1)} %collective-permute-done.13.refs_1_, bf16[7168,2048]{1,0:T(8,128)(2,1)} %refs_2_.29, f32[256,2048]{1,0:T(8,128)S(1)} %last_dot.6.refs_2_.refs_3_, ...), custom_call_target="tpu_custom_call" | custom-call | flops 3758096384 | bytes 14680064 | tf_op jit(solution)/shard_map/last_dot/pallas_call | solution.py:225
  269.8 8.0 %all_gather.59.refs_0_ = bf16[2,32,3584]{2,1,0:T(8,128)(2,1)S(1)} all-gather(bf16[1,32,3584]{2,1,0:T(8,128)(2,1)S(1)} %activate.8.refs_4_), channel_id=1, replica_groups={{0,8},{4,12},{1,9},{5,13},{2,10},{6,14},{3,11},{7,15},{16,24},{20,28},{..., dimensions={0}, use_global_device_ids=true | all-gather | bytes 688128 | tf_op jit(solution)/shard_map/all_gather | solution.py:266
  277.7 13.6 %all_gather.57.refs_1_ = bf16[4,32,3584]{2,1,0:T(8,128)(2,1)S(1)} all-gather(bf16[2,32,3584]{2,1,0:T(8,128)(2,1)S(1)} %get-tuple-element.84.refs_3_), channel_id=1, replica_groups={{0,8},{4,12},{1,9},{5,13},{2,10},{6,14},{3,11},{7,15},{16,24},{20,28},{..., dimensions={0}, use_global_device_ids=true | all-gather | bytes 1376256 | tf_op jit(solution)/shard_map/all_gather | solution.py:266
  291.6 7.9 %all_gather.58.refs_0_ = bf16[2,32,3584]{2,1,0:T(8,128)(2,1)S(1)} all-gather(bf16[1,32,3584]{2,1,0:T(8,128)(2,1)S(1)} %activate.9.refs_3_), channel_id=1, replica_groups={{0,8},{4,12},{1,9},{5,13},{2,10},{6,14},{3,11},{7,15},{16,24},{20,28},{..., dimensions={0}, use_global_device_ids=true | all-gather | bytes 688128 | tf_op jit(solution)/shard_map/all_gather | solution.py:266
  299.7 6.1 %last_dot.8.refs_3_.refs_4_ = f32[128,2048]{1,0:T(8,128)S(1)} custom-call(bf16[2,32,3584]{2,1,0:T(8,128)(2,1)S(1)} %all_gather.59.refs_0_, bf16[2,32,3584]{2,1,0:T(8,128)(2,1)S(1)} %collective-permute-done.19.refs_1_, bf16[7168,2048]{1,0:T(8,128)(2,1)} %refs_2_.29, bf16[1,32,3584]{2,1,0:T(8,128)(2,1)S(1)} %activate.9.refs_3_), custom_call_target="tpu_custom_call" | custom-call | flops 1879048192 | bytes 14680064 | tf_op jit(solution)/shard_map/last_dot/pallas_call | solution.py:225
  305.8 6.0 %last_dot.9 = bf16[128,2048]{1,0:T(8,128)(2,1)S(1)} custom-call(bf16[2,32,3584]{2,1,0:T(8,128)(2,1)S(1)} %all_gather.58.refs_0_, bf16[2,32,3584]{2,1,0:T(8,128)(2,1)S(1)} %collective-permute-done.18.refs_1_, bf16[7168,2048]{1,0:T(8,128)(2,1)} %refs_2_.29, f32[128,2048]{1,0:T(8,128)S(1)} %last_dot.8.refs_3_.refs_4_, f32[128,2048]{1,0:T(8,128)S(1)} %last_dot.8.refs_3_.refs_4_), custom_call_target="tpu_custom_call" | custom-call | flops 1879048192 | bytes 14680064 | tf_op jit(solution)/shard_map/last_dot/pallas_call | solution.py:225
  311.8 4.0 %collective-permute-done.17 = bf16[128,2048]{1,0:T(8,128)(2,1)S(1)} collective-permute-done((bf16[128,2048]{1,0:T(8,128)(2,1)S(1)}, bf16[128,2048]{1,0:T(8,128)(2,1)S(1)}, u32[]{:S(2)}, u32[]{:S(2)}) %collective-permute-start.17) | collective-permute-done | bytes 524320 | tf_op jit(solution)/shard_map/ppermute | solution.py:260
  316.0 15.3 %collective-permute-done.20 = bf16[128,2048]{1,0:T(8,128)(2,1)S(1)} collective-permute-done((bf16[128,2048]{1,0:T(8,128)(2,1)S(1)}, bf16[128,2048]{1,0:T(8,128)(2,1)S(1)}, u32[]{:S(2)}, u32[]{:S(2)}) %collective-permute-start.20) | collective-permute-done | bytes 524320 | tf_op jit(solution)/shard_map/ppermute | solution.py:260
  331.4 1.0 add_convert_fusion
  (104 shorter events, 6.3 us)
Async XLA Ops:
  6.5 166.4 %all-gather.5.cloned.1.call-start = ((), (), s32[]{:S(2)}) async-start(), calls=%async_computation.1 | async-start | bytes 1572864 | tf_op jit(solution)/shard_map/all_gather | solution.py:266
  6.5 17.2 %collective-permute-start = (bf16[128,2048]{1,0:T(8,128)(2,1)}, bf16[128,2048]{1,0:T(8,128)(2,1)S(1)}, u32[]{:S(2)}, u32[]{:S(2)}) collective-permute-start(bf16[128,2048]{1,0:T(8,128)(2,1)} %refs_0_.7), channel_id=1, source_target_pairs={{0,1},{1,2},{2,3},{3,0},{4,5},{5,6},{6,7},{7,4},{8,9},{9,10},{10,1... | collective-permute-start | bytes 1572872 | tf_op jit(solution)/shard_map/ppermute | solution.py:260
  9.6 1.1 copy-start
  15.9 7.2 %collective-permute-start.2 = (bf16[2,64,1536]{2,1,0:T(8,128)(2,1)S(1)}, bf16[2,64,1536]{2,1,0:T(8,128)(2,1)S(1)}, u32[]{:S(2)}, u32[]{:S(2)}) collective-permute-start(bf16[2,64,1536]{2,1,0:T(8,128)(2,1)S(1)} %get-tuple-element.48.refs_3_), channel_id=1, source_target_pairs={{0,4},{4,0},{8,12},{12,8},{1,5},{5,1},{9,13},{13,9},{2,6},{6,2},{1... | collective-permute-start | bytes 1179656 | tf_op jit(solution)/shard_map/ppermute | solution.py:263
  22.6 7.8 %collective-permute-start.4 = (bf16[2,64,2048]{2,1,0:T(8,128)(2,1)S(1)}, bf16[2,64,2048]{2,1,0:T(8,128)(2,1)S(1)}, u32[]{:S(2)}, u32[]{:S(2)}) collective-permute-start(bf16[2,64,2048]{2,1,0:T(8,128)(2,1)S(1)} %get-tuple-element.49.refs_2_), channel_id=1, source_target_pairs={{0,4},{4,0},{8,12},{12,8},{1,5},{5,1},{9,13},{13,9},{2,6},{6,2},{1... | collective-permute-start | bytes 1572872 | tf_op jit(solution)/shard_map/ppermute | solution.py:263
  23.4 7.0 %copy-start.33 = (bf16[2,32,1536]{2,1,0:T(8,128)(2,1)}, bf16[2,32,1536]{2,1,0:T(8,128)(2,1)S(1)}, u32[]{:S(2)}) copy-start(bf16[2,32,1536]{2,1,0:T(8,128)(2,1)S(1)} %get-tuple-element.65.refs_0_) | copy-start | bytes 589828
  23.7 15.4 %collective-permute-start.1 = (bf16[128,2048]{1,0:T(8,128)(2,1)S(1)}, bf16[128,2048]{1,0:T(8,128)(2,1)S(1)}, u32[]{:S(2)}, u32[]{:S(2)}) collective-permute-start(bf16[128,2048]{1,0:T(8,128)(2,1)S(1)} %collective-permute-done.refs_0_), channel_id=1, source_target_pairs={{0,1},{1,2},{2,3},{3,0},{4,5},{5,6},{6,7},{7,4},{8,9},{9,10},{10,1... | collective-permute-start | bytes 1572872 | tf_op jit(solution)/shard_map/ppermute | solution.py:260
  30.3 7.6 %collective-permute-start.3 = (bf16[2,64,1536]{2,1,0:T(8,128)(2,1)S(1)}, bf16[2,64,1536]{2,1,0:T(8,128)(2,1)S(1)}, u32[]{:S(2)}, u32[]{:S(2)}) collective-permute-start(bf16[2,64,1536]{2,1,0:T(8,128)(2,1)S(1)} %get-tuple-element.52.refs_2_), channel_id=1, source_target_pairs={{0,4},{4,0},{8,12},{12,8},{1,5},{5,1},{9,13},{13,9},{2,6},{6,2},{1... | collective-permute-start | bytes 1179656 | tf_op jit(solution)/shard_map/ppermute | solution.py:263
  30.7 6.7 %copy-start.29 = (bf16[2,32,2048]{2,1,0:T(8,128)(2,1)}, bf16[2,32,2048]{2,1,0:T(8,128)(2,1)S(1)}, u32[]{:S(2)}) copy-start(bf16[2,32,2048]{2,1,0:T(8,128)(2,1)S(1)} %get-tuple-element.66.refs_2_) | copy-start | bytes 786436
  37.4 7.9 %collective-permute-start.6 = (bf16[2,64,2048]{2,1,0:T(8,128)(2,1)S(1)}, bf16[2,64,2048]{2,1,0:T(8,128)(2,1)S(1)}, u32[]{:S(2)}, u32[]{:S(2)}) collective-permute-start(bf16[2,64,2048]{2,1,0:T(8,128)(2,1)S(1)} %get-tuple-element.55.refs_2_), channel_id=1, source_target_pairs={{0,4},{4,0},{8,12},{12,8},{1,5},{5,1},{9,13},{13,9},{2,6},{6,2},{1... | collective-permute-start | bytes 1572872 | tf_op jit(solution)/shard_map/ppermute | solution.py:263
  38.2 0.7 copy-start.35
  45.2 39.7 %collective-permute-start.5 = (bf16[2,128,1536]{2,1,0:T(8,128)(2,1)S(1)}, bf16[2,128,1536]{2,1,0:T(8,128)(2,1)S(1)}, u32[]{:S(2)}, u32[]{:S(2)}) collective-permute-start(bf16[2,128,1536]{2,1,0:T(8,128)(2,1)S(1)} %get-tuple-element.58.refs_2_), channel_id=1, source_target_pairs={{0,4},{4,0},{8,12},{12,8},{1,5},{5,1},{9,13},{13,9},{2,6},{6,2},{1... | collective-permute-start | bytes 2359304 | tf_op jit(solution)/shard_map/ppermute | solution.py:263
  45.6 0.7 copy-start.31
  53.9 38.7 %collective-permute-start.8 = (bf16[2,128,2048]{2,1,0:T(8,128)(2,1)S(1)}, bf16[2,128,2048]{2,1,0:T(8,128)(2,1)S(1)}, u32[]{:S(2)}, u32[]{:S(2)}) collective-permute-start(bf16[2,128,2048]{2,1,0:T(8,128)(2,1)S(1)} %get-tuple-element.61.refs_2_), channel_id=1, source_target_pairs={{0,4},{4,0},{8,12},{12,8},{1,5},{5,1},{9,13},{13,9},{2,6},{6,2},{1... | collective-permute-start | bytes 3145736 | tf_op jit(solution)/shard_map/ppermute | solution.py:263
  76.5 52.4 %collective-permute-start.10 = (bf16[128,2048]{1,0:T(8,128)(2,1)S(1)}, bf16[128,2048]{1,0:T(8,128)(2,1)S(1)}, u32[]{:S(2)}, u32[]{:S(2)}) collective-permute-start(bf16[128,2048]{1,0:T(8,128)(2,1)S(1)} %collective-permute-done.1.refs_1_), channel_id=1, source_target_pairs={{0,1},{1,2},{2,3},{3,0},{4,5},{5,6},{6,7},{7,4},{8,9},{9,10},{10,1... | collective-permute-start | bytes 1572872 | tf_op jit(solution)/shard_map/ppermute | solution.py:260
  85.3 7.1 %copy-start.5 = (bf16[2,64,1536]{2,1,0:T(8,128)(2,1)}, bf16[2,64,1536]{2,1,0:T(8,128)(2,1)S(1)}, u32[]{:S(2)}) copy-start(bf16[2,64,1536]{2,1,0:T(8,128)(2,1)S(1)} %get-tuple-element.62.refs_4_) | copy-start | bytes 1179652
  85.3 7.1 %copy-start.25 = (bf16[2,64,1536]{2,1,0:T(8,128)(2,1)}, bf16[2,64,1536]{2,1,0:T(8,128)(2,1)S(1)}, u32[]{:S(2)}) copy-start(bf16[2,64,1536]{2,1,0:T(8,128)(2,1)S(1)} %get-tuple-element.79.refs_0_) | copy-start | bytes 1179652
  85.3 9.2 %copy-start.7 = (bf16[4,32,1536]{2,1,0:T(8,128)(2,1)S(1)}, bf16[4,32,1536]{2,1,0:T(8,128)(2,1)}, u32[]{:S(2)}) copy-start(bf16[4,32,1536]{2,1,0:T(8,128)(2,1)} %all_gather.45.refs_1_) | copy-start | bytes 1179652
  92.4 1.3 copy-start.17
  92.5 33.3 %collective-permute-start.7 = (bf16[2,128,1536]{2,1,0:T(8,128)(2,1)}, bf16[2,128,1536]{2,1,0:T(8,128)(2,1)}, u32[]{:S(2)}, u32[]{:S(2)}) collective-permute-start(bf16[2,128,1536]{2,1,0:T(8,128)(2,1)} %get-tuple-element.64.refs_2_), channel_id=1, source_target_pairs={{0,4},{4,0},{8,12},{12,8},{1,5},{5,1},{9,13},{13,9},{2,6},{6,2},{1... | collective-permute-start | bytes 2359304 | tf_op jit(solution)/shard_map/ppermute | solution.py:263
  93.7 0.8 copy-start.19
  94.5 1.0 copy-start.8
  95.5 0.9 copy-start.30
  96.5 0.9 copy-start.32
  97.4 0.9 copy-start.34
  98.4 0.9 copy-start.36
  108.0 32.6 %copy-start.11 = (bf16[2,128,2048]{2,1,0:T(8,128)(2,1)}, bf16[2,128,2048]{2,1,0:T(8,128)(2,1)S(1)}, u32[]{:S(2)}) copy-start(bf16[2,128,2048]{2,1,0:T(8,128)(2,1)S(1)} %get-tuple-element.74.refs_0_) | copy-start | bytes 3145732
  108.0 45.6 %collective-permute-start.9 = (bf16[2,128,2048]{2,1,0:T(8,128)(2,1)}, bf16[2,128,2048]{2,1,0:T(8,128)(2,1)}, u32[]{:S(2)}, u32[]{:S(2)}) collective-permute-start(bf16[2,128,2048]{2,1,0:T(8,128)(2,1)} %get-tuple-element.71.refs_2_), channel_id=1, source_target_pairs={{0,4},{4,0},{8,12},{12,8},{1,5},{5,1},{9,13},{13,9},{2,6},{6,2},{1... | collective-permute-start | bytes 3145736 | tf_op jit(solution)/shard_map/ppermute | solution.py:263
  108.6 110.5 %all-gather.3.cloned.1.call-start = ((), (), s32[]{:S(2)}) async-start(), calls=%async_computation | async-start | bytes 1572864 | tf_op jit(solution)/shard_map/all_gather | solution.py:266
  125.8 80.7 %collective-permute-start.11 = (bf16[2,32,7168]{2,1,0:T(8,128)(2,1)S(1)}, bf16[2,32,7168]{2,1,0:T(8,128)(2,1)}, u32[]{:S(2)}, u32[]{:S(2)}) collective-permute-start(bf16[2,32,7168]{2,1,0:T(8,128)(2,1)S(1)} %all_gather.51.refs_0_), channel_id=1, source_target_pairs={{0,4},{4,0},{8,12},{12,8},{1,5},{5,1},{9,13},{13,9},{2,6},{6,2},{1... | collective-permute-start | bytes 2752520 | tf_op jit(solution)/shard_map/ppermute | solution.py:263
  125.8 1.1 copy-start.18
  128.2 0.7 copy-start.27
  129.0 11.6 %copy-start.2 = (bf16[128,2048]{1,0:T(8,128)(2,1)}, bf16[128,2048]{1,0:T(8,128)(2,1)S(1)}, u32[]{:S(2)}) copy-start(bf16[128,2048]{1,0:T(8,128)(2,1)S(1)} %collective-permute-done.10.refs_0_) | copy-start | bytes 1572868
  129.0 12.2 %copy-start.6 = (bf16[2,64,1536]{2,1,0:T(8,128)(2,1)S(1)}, bf16[2,64,1536]{2,1,0:T(8,128)(2,1)}, u32[]{:S(2)}) copy-start(bf16[2,64,1536]{2,1,0:T(8,128)(2,1)} %copy-done.5) | copy-start | bytes 1179652
  129.0 44.0 %copy-start.20 = (bf16[2,64,2048]{2,1,0:T(8,128)(2,1)S(1)}, bf16[2,64,2048]{2,1,0:T(8,128)(2,1)}, u32[]{:S(2)}) copy-start(bf16[2,64,2048]{2,1,0:T(8,128)(2,1)} %copy-done.19) | copy-start | bytes 1572868
  140.6 16.4 %copy-start.15 = (bf16[2,64,3584]{2,1,0:T(8,128)(2,1)}, bf16[2,64,3584]{2,1,0:T(8,128)(2,1)S(1)}, u32[]{:S(2)}) copy-start(bf16[2,64,3584]{2,1,0:T(8,128)(2,1)S(1)} %get-tuple-element.78.refs_0_) | copy-start | bytes 2752516
  140.6 62.8 %collective-permute-start.12 = (bf16[2,64,3584]{2,1,0:T(8,128)(2,1)}, bf16[2,64,3584]{2,1,0:T(8,128)(2,1)}, u32[]{:S(2)}, u32[]{:S(2)}) collective-permute-start(bf16[2,64,3584]{2,1,0:T(8,128)(2,1)} %get-tuple-element.75.refs_2_), channel_id=1, source_target_pairs={{0,4},{4,0},{8,12},{12,8},{1,5},{5,1},{9,13},{13,9},{2,6},{6,2},{1... | collective-permute-start | bytes 2752520 | tf_op jit(solution)/shard_map/ppermute | solution.py:263
  153.6 1.2 copy-start.12
  156.9 0.8 copy-start.21
  173.0 1.2 copy-start.9
  174.2 1.0 copy-start.26
  175.6 1.0 copy-start.3
  176.7 26.8 %copy-start.16 = (bf16[2,64,3584]{2,1,0:T(8,128)(2,1)S(1)}, bf16[2,64,3584]{2,1,0:T(8,128)(2,1)}, u32[]{:S(2)}) copy-start(bf16[2,64,3584]{2,1,0:T(8,128)(2,1)} %copy-done.15) | copy-start | bytes 2752516
  188.1 1.0 copy-start.13
  189.1 30.0 %copy-start.28 = (bf16[2,64,1536]{2,1,0:T(8,128)(2,1)S(1)}, bf16[2,64,1536]{2,1,0:T(8,128)(2,1)}, u32[]{:S(2)}) copy-start(bf16[2,64,1536]{2,1,0:T(8,128)(2,1)} %copy-done.27) | copy-start | bytes 1179652
  189.1 60.1 %collective-permute-start.15 = (bf16[2,64,3584]{2,1,0:T(8,128)(2,1)}, bf16[2,64,3584]{2,1,0:T(8,128)(2,1)}, u32[]{:S(2)}, u32[]{:S(2)}) collective-permute-start(bf16[2,64,3584]{2,1,0:T(8,128)(2,1)} %get-tuple-element.81.refs_2_), channel_id=1, source_target_pairs={{0,4},{4,0},{8,12},{12,8},{1,5},{5,1},{9,13},{13,9},{2,6},{6,2},{1... | collective-permute-start | bytes 2752520 | tf_op jit(solution)/shard_map/ppermute | solution.py:263
  203.4 49.2 %collective-permute-start.14 = (bf16[2,64,3584]{2,1,0:T(8,128)(2,1)S(1)}, bf16[2,64,3584]{2,1,0:T(8,128)(2,1)}, u32[]{:S(2)}, u32[]{:S(2)}) collective-permute-start(bf16[2,64,3584]{2,1,0:T(8,128)(2,1)S(1)} %all_gather.55.refs_0_), channel_id=1, source_target_pairs={{0,4},{4,0},{8,12},{12,8},{1,5},{5,1},{9,13},{13,9},{2,6},{6,2},{1... | collective-permute-start | bytes 2752520 | tf_op jit(solution)/shard_map/ppermute | solution.py:263
  205.7 0.8 copy-start.23
  218.3 0.8 copy-start.4
  219.1 1.2 copy-start.10
  220.3 1.0 copy-start.22
  235.4 27.5 %collective-permute-start.13 = (bf16[2,64,3584]{2,1,0:T(8,128)(2,1)S(1)}, bf16[2,64,3584]{2,1,0:T(8,128)(2,1)S(1)}, u32[]{:S(2)}, u32[]{:S(2)}) collective-permute-start(bf16[2,64,3584]{2,1,0:T(8,128)(2,1)S(1)} %all_gather.54.refs_0_), channel_id=1, source_target_pairs={{0,4},{4,0},{8,12},{12,8},{1,5},{5,1},{9,13},{13,9},{2,6},{6,2},{1... | collective-permute-start | bytes 2752520 | tf_op jit(solution)/shard_map/ppermute | solution.py:263
  249.2 1.2 copy-start.14
  261.6 1.0 copy-start.24
  269.7 29.8 %collective-permute-start.16 = (bf16[128,2048]{1,0:T(8,128)(2,1)S(1)}, bf16[128,2048]{1,0:T(8,128)(2,1)S(1)}, u32[]{:S(2)}, u32[]{:S(2)}) collective-permute-start(bf16[128,2048]{1,0:T(8,128)(2,1)S(1)} %get-tuple-element.86.refs_2_), channel_id=1, source_target_pairs={{0,1},{1,2},{2,3},{3,0},{4,5},{5,6},{6,7},{7,4},{8,9},{9,10},{10,1... | collective-permute-start | bytes 1572872 | tf_op jit(solution)/shard_map/ppermute | solution.py:260
  277.7 22.0 %collective-permute-start.19 = (bf16[2,32,3584]{2,1,0:T(8,128)(2,1)S(1)}, bf16[2,32,3584]{2,1,0:T(8,128)(2,1)S(1)}, u32[]{:S(2)}, u32[]{:S(2)}) collective-permute-start(bf16[2,32,3584]{2,1,0:T(8,128)(2,1)S(1)} %all_gather.59.refs_0_), channel_id=1, source_target_pairs={{0,4},{4,0},{8,12},{12,8},{1,5},{5,1},{9,13},{13,9},{2,6},{6,2},{1... | collective-permute-start | bytes 1376264 | tf_op jit(solution)/shard_map/ppermute | solution.py:263
  299.5 6.3 %collective-permute-start.18 = (bf16[2,32,3584]{2,1,0:T(8,128)(2,1)S(1)}, bf16[2,32,3584]{2,1,0:T(8,128)(2,1)S(1)}, u32[]{:S(2)}, u32[]{:S(2)}) collective-permute-start(bf16[2,32,3584]{2,1,0:T(8,128)(2,1)S(1)} %all_gather.58.refs_0_), channel_id=1, source_target_pairs={{0,4},{4,0},{8,12},{12,8},{1,5},{5,1},{9,13},{13,9},{2,6},{6,2},{1... | collective-permute-start | bytes 1376264 | tf_op jit(solution)/shard_map/ppermute | solution.py:263
  299.6 31.7 %copy-start.1 = (bf16[128,2048]{1,0:T(8,128)(2,1)S(1)}, bf16[128,2048]{1,0:T(8,128)(2,1)}, u32[]{:S(2)}) copy-start(bf16[128,2048]{1,0:T(8,128)(2,1)} %refs_0_.7) | copy-start | bytes 1572868
  299.6 16.2 %collective-permute-start.17 = (bf16[128,2048]{1,0:T(8,128)(2,1)S(1)}, bf16[128,2048]{1,0:T(8,128)(2,1)S(1)}, u32[]{:S(2)}, u32[]{:S(2)}) collective-permute-start(bf16[128,2048]{1,0:T(8,128)(2,1)S(1)} %add_convert_fusion.2), channel_id=1, source_target_pairs={{0,1},{1,2},{2,3},{3,0},{4,5},{5,6},{6,7},{7,4},{8,9},{9,10},{10,1... | collective-permute-start | bytes 1572872 | tf_op jit(solution)/shard_map/ppermute | solution.py:260
  315.9 15.4 %collective-permute-start.20 = (bf16[128,2048]{1,0:T(8,128)(2,1)S(1)}, bf16[128,2048]{1,0:T(8,128)(2,1)S(1)}, u32[]{:S(2)}, u32[]{:S(2)}) collective-permute-start(bf16[128,2048]{1,0:T(8,128)(2,1)S(1)} %add_convert_fusion.1), channel_id=1, source_target_pairs={{0,1},{1,2},{2,3},{3,0},{4,5},{5,6},{6,7},{7,4},{8,9},{9,10},{10,1... | collective-permute-start | bytes 1572872 | tf_op jit(solution)/shard_map/ppermute | solution.py:260
Sparse Core Ops, SparseCore 0:
  108.7 24.5 all-gather.4
  157.9 22.7 all-gather.2
